TPU v7x, 256 devices: a whole 4x4x8 slice. The times are simulated.
256 devices in a mesh: grp: 16 (over z, y_hi), ep: 16 (over y_lo, x, core).
Axes of the slice: x: 4, y: 4 (y_hi: 2, y_lo: 2; y = y_hi * 2 + y_lo), z: 8, core: 2. Of those that a mesh axis runs over, the one named last changes fastest.
Arguments:
- tokens: bfloat16 [49152, 4096], P(('grp', 'ep')), may hold values from -6 to 6
- expert_ids: int32 [49152, 8], P(('grp', 'ep')), may hold values from 0 to 127, all different within a row; in each aligned block of 192 rows (0 to 191, 192 to 383, ...) at most 24 rows name the same one
- gate_probs: float32 [49152, 8], P(('grp', 'ep')), may hold values from 0.02 to 0.25
- placement: int32 [16, 4], P('grp'), may hold values from 0 to 1
- gate_weight: bfloat16 [16, 4096, 3072], P('grp', None, 'ep'), may hold values from -0.09375 to 0.09375
- up_weight: bfloat16 [16, 4096, 3072], P('grp', None, 'ep'), may hold values from -0.09375 to 0.09375
- down_weight: bfloat16 [16, 3072, 4096], P('grp', 'ep'), may hold values from -0.21875 to 0.21875
- out_grad: bfloat16 [49152, 4096], P(('grp', 'ep')), may hold values from -6 to 6
- moment_first: float32 [2, 3072, 4096], P(None, 'ep', 'grp'), may hold values from -2 to 2
- moment_second: float32 [2, 3072, 4096], P(None, 'ep', 'grp'), may hold values from 0.01 to 1
Outputs:
- token_grad: bfloat16 [49152, 4096], P(('grp', 'ep'))
- step_dir: bfloat16 [16, 3072, 4096], P('grp', 'ep')
- new_first: float32 [2, 3072, 4096], P(None, 'ep', 'grp')
- new_second: float32 [2, 3072, 4096], P(None, 'ep', 'grp')
Inputs may be any that keep to these rules, and one draw needn't show every extreme that they name: `expert_ids`: each row names 8 different experts. In the rows of one device no expert is named more than 24 times, a bound that some block reaches. Group g holds expert placement[g, s] * 4 + s in its slot s.
All inputs are finite; a program needn't handle non-finite values.
Results may differ from a plain program's by a relative error of at most 0.015.
Values may be sent and summed in bfloat16 or wider, within the bound.
A program may use at most 128 MiB of HBM per device.

v0:
```python
import math
import jax
import jax.numpy as jnp
from jax import lax
from jax.sharding import PartitionSpec as P

QUARTERS = 4
CANDS = 2
CAP = 24
beta_one = 0.9
beta_two = 0.999
adam_eps = 1e-08
first_fix = 1.0 - math.exp(1000.0 * math.log(0.9))
second_fix = 1.0 - math.exp(1000.0 * math.log(0.999))


def moments(gradient, first_moment, second):
    new_first = beta_one * first_moment + (1.0 - beta_one) * gradient
    new_second = beta_two * second + (1.0 - beta_two) * gradient * gradient
    return (new_first, new_second)


def direction(new_first, new_second):
    return new_first / first_fix / (jnp.sqrt(new_second / second_fix) + adam_eps)


def body(
    tokens,
    expert_ids,
    gate_probs,
    placement,
    gate_weight,
    up_weight,
    down_weight,
    out_grad,
    moment_first,
    moment_second,
):
    num_ep = lax.axis_size("ep")
    slot_count = num_ep // QUARTERS
    tok_count = tokens.shape[0]
    width = tokens.shape[1]
    held_ids = placement[0] * slot_count + jnp.arange(slot_count, dtype=jnp.int32)
    matches = expert_ids[:, :, None] == held_ids[None, None, :]
    hit_rows = jnp.any(matches, axis=1)
    coeffs = jnp.sum(jnp.where(matches, gate_probs[:, :, None], jnp.float32(0.0)), axis=1)
    ranking = jnp.cumsum(hit_rows.astype(jnp.int32), axis=0) - 1
    select_mask = hit_rows.T[:, None, :] & (
        ranking.T[:, None, :] == jnp.arange(CAP, dtype=jnp.int32)[None, :, None]
    )
    select_flat = select_mask.reshape(slot_count * CAP, tok_count).astype(jnp.bfloat16)
    send_tokens = jnp.dot(select_flat, tokens, preferred_element_type=jnp.float32).astype(
        jnp.bfloat16
    )
    send_grads = jnp.dot(select_flat, out_grad, preferred_element_type=jnp.float32).astype(
        jnp.bfloat16
    )
    send_coeffs = jnp.sum(select_mask.astype(jnp.float32) * coeffs.T[:, None, :], axis=2)

    def spread(source):
        shaped = source.reshape(slot_count, 1, CAP, width)
        return jnp.broadcast_to(shaped, (slot_count, QUARTERS, CAP, width)).reshape(
            num_ep, CAP, width
        )

    coeff_spread = jnp.broadcast_to(send_coeffs[:, None, :], (slot_count, QUARTERS, CAP)).reshape(
        num_ep, CAP
    )
    w_gate = gate_weight[0]
    w_up = up_weight[0]
    w_down = down_weight[0]
    recv_tokens, recv_grads, recv_coeffs = (
        lax.all_to_all(spread(send_tokens), "ep", split_axis=0, concat_axis=0, tiled=True),
        lax.all_to_all(spread(send_grads), "ep", split_axis=0, concat_axis=0, tiled=True),
        lax.all_to_all(
            coeff_spread.astype(jnp.bfloat16), "ep", split_axis=0, concat_axis=0, tiled=True
        ).astype(coeff_spread.dtype),
    )
    in_rows = recv_tokens.reshape(num_ep * CAP, width)
    pre_gate = jnp.dot(in_rows, w_gate, preferred_element_type=jnp.float32)
    pre_up = jnp.dot(in_rows, w_up, preferred_element_type=jnp.float32)
    sigmoid_gate = jax.nn.sigmoid(pre_gate)
    activated = pre_gate * sigmoid_gate
    hidden = (activated * pre_up).astype(jnp.bfloat16)
    pre_gate, pre_up, sigmoid_gate, activated, hidden = (
        pre_gate,
        pre_up,
        sigmoid_gate,
        activated,
        hidden,
    )
    scaled = (
        recv_coeffs.reshape(num_ep * CAP)[:, None]
        * recv_grads.reshape(num_ep * CAP, width).astype(jnp.float32)
    ).astype(jnp.bfloat16)
    d_hidden = jnp.einsum("rd,hd->rh", scaled, w_down, preferred_element_type=jnp.float32)
    weight_grad = jnp.einsum("rh,rd->hd", hidden, scaled, preferred_element_type=jnp.float32)
    d_gate = (d_hidden * pre_up * sigmoid_gate * (1.0 + pre_gate * (1.0 - sigmoid_gate))).astype(
        jnp.bfloat16
    )
    d_up = (d_hidden * activated).astype(jnp.bfloat16)
    partial_value = jnp.einsum("rh,dh->rd", d_gate, w_gate, preferred_element_type=jnp.float32)
    partial_value = (
        partial_value + jnp.einsum("rh,dh->rd", d_up, w_up, preferred_element_type=jnp.float32)
    ).astype(jnp.bfloat16)
    returned = lax.all_to_all(
        partial_value.reshape(num_ep, CAP, width), "ep", split_axis=0, concat_axis=0, tiled=True
    )
    combine = jnp.broadcast_to(
        select_mask.reshape(slot_count, 1, CAP, tok_count), (slot_count, QUARTERS, CAP, tok_count)
    )
    combine = combine.reshape(num_ep * CAP, tok_count).astype(jnp.bfloat16)
    token_grad = jnp.einsum(
        "kt,kd->td",
        combine,
        returned.reshape(num_ep * CAP, width),
        preferred_element_type=jnp.float32,
    ).astype(jnp.bfloat16)
    ep_index = lax.axis_index("ep")
    my_cand = lax.dynamic_index_in_dim(placement[0], ep_index // QUARTERS, 0, keepdims=False)
    cand_mask = (jnp.arange(CANDS, dtype=jnp.int32) == my_cand).astype(jnp.float32)
    cand_grads = cand_mask[:, None, None] * weight_grad[None]
    totals = lax.psum(cand_grads.astype(jnp.bfloat16), "grp").astype(jnp.float32)
    full_first, full_second = (
        lax.all_gather(moment_first.astype(jnp.bfloat16), "grp", axis=2, tiled=True).astype(
            moment_first.dtype
        ),
        lax.all_gather(moment_second.astype(jnp.bfloat16), "grp", axis=2, tiled=True).astype(
            moment_second.dtype
        ),
    )
    share_cols = moment_first.shape[2]
    share_start = lax.axis_index("grp") * share_cols
    new_first, new_second = moments(
        lax.dynamic_slice_in_dim(totals, share_start, share_cols, 2), moment_first, moment_second
    )
    own_grad = lax.dynamic_index_in_dim(totals, my_cand, 0, keepdims=True)
    own_first = lax.dynamic_index_in_dim(full_first, my_cand, 0, keepdims=True)
    own_second = lax.dynamic_index_in_dim(full_second, my_cand, 0, keepdims=True)
    copy_first, copy_second = moments(own_grad, own_first, own_second)
    step_dir = direction(copy_first, copy_second).astype(jnp.bfloat16)
    return (token_grad, step_dir, new_first, new_second)


def solution(mesh):
    return jax.shard_map(
        body,
        mesh=mesh,
        in_specs=(
            P(("grp", "ep"), None),
            P(("grp", "ep"), None),
            P(("grp", "ep"), None),
            P("grp", None),
            P("grp", None, "ep"),
            P("grp", None, "ep"),
            P("grp", "ep", None),
            P(("grp", "ep"), None),
            P(None, "ep", "grp"),
            P(None, "ep", "grp"),
        ),
        out_specs=(
            P(("grp", "ep"), None),
            P("grp", "ep", None),
            P(None, "ep", "grp"),
            P(None, "ep", "grp"),
        ),
        check_vma=False,
    )
```

profile of v0, /device:TPU:2, one launch (start us, length us, event | category | flops | bytes accessed | tf_op | source)
XLA Modules:
  0.0 527.4 jit_solution(9174069582011565920)
XLA Ops:
  7.2 0.0 copy-start
  7.2 0.8 bitcast_add_fusion
  8.0 0.8 compare_reduce_fusion
  8.7 0.8 fusion.24
  9.6 1.2 reduce-window.6
  10.8 0.1 slice.12
  10.9 0.1 copy.27
  11.0 0.1 copy.28
  11.1 0.1 add_bitcast_fusion
  11.2 0.1 select_reduce_fusion
  11.3 0.6 copy.29
  11.9 5.9 %all-to-all-start = ((bf16[16,1,24]{2,1,0:T(2,128)(2,1)}), bf16[16,1,24]{2,1,0:T(2,128)(2,1)S(1)}, u32[]{:S(2)}, u32[]{:S(2)}) async-start(bf16[16,1,24]{2,1,0:T(2,128)(2,1)} %copy.29), calls=%async_computation | async-start | bytes 16384 | tf_op jit(solution)/shard_map/all_to_all | solution.py:75
  17.8 0.1 eq.59
  17.9 0.1 fusion.21
  18.0 1.8 convolution_convert_fusion.1
  19.8 2.6 all-to-all-done
  22.4 2.1 broadcast_in_dim.53
  24.5 5.7 %all-to-all-start.2 = ((bf16[16,24,4096]{2,1,0:T(8,128)(2,1)}), bf16[16,24,4096]{2,1,0:T(8,128)(2,1)}, u32[]{:S(2)}, u32[]{:S(2)}) async-start(bf16[16,24,4096]{2,1,0:T(8,128)(2,1)} %bitcast.62), calls=%async_computation.2 | async-start | bytes 6291456 | tf_op jit(solution)/shard_map/all_to_all | solution.py:73
  30.2 1.8 convolution_convert_fusion.2
  31.9 41.2 %all-to-all-done.2 = bf16[16,24,4096]{2,1,0:T(8,128)(2,1)} async-done(((bf16[16,24,4096]{2,1,0:T(8,128)(2,1)}), bf16[16,24,4096]{2,1,0:T(8,128)(2,1)}, u32[]{:S(2)}, u32[]{:S(2)}) %all-to-all-start.2) | async-done | bytes 3145760 | tf_op jit(solution)/shard_map/all_to_all | solution.py:73
  73.1 2.1 broadcast_in_dim.29
  75.1 0.0 copy-start.8
  75.2 4.5 all-to-all-start.1
  79.7 0.0 copy-start.2
  79.7 0.0 all-reduce.3.cloned.1.call-start
  79.8 0.0 copy-done.8
  79.8 0.6 constant_dynamic-slice_fusion
  80.4 0.6 compare_convert_fusion
  81.0 0.1 reshape.120
  81.1 0.0 copy-done
  81.1 3.1 fusion.9
  84.2 0.0 copy-done.2
  84.2 3.8 fusion.12
  88.0 34.3 %all-to-all-done.1 = bf16[16,24,4096]{2,1,0:T(8,128)(2,1)} async-done(((bf16[16,24,4096]{2,1,0:T(8,128)(2,1)}), bf16[16,24,4096]{2,1,0:T(8,128)(2,1)}, u32[]{:S(2)}, u32[]{:S(2)}) %all-to-all-start.1) | async-done | bytes 3145760 | tf_op jit(solution)/shard_map/all_to_all | solution.py:74
  122.3 2.9 fusion
  125.2 0.0 copy-done.3
  125.3 1.0 fusion.18
  126.3 2.3 multiply_convert_fusion
  128.5 0.0 all-reduce.3.cloned.1.call-update
  128.5 0.0 all-gather.3.cloned.1.call-start
  128.6 181.3 %all-reduce.3.cloned.1.call-done = bf16[2,192,4096]{2,1,0:T(8,128)(2,1)} async-done(((bf16[2,192,4096]{2,1,0:T(8,128)(2,1)}), bf16[2,192,4096]{2,1,0:T(8,128)(2,1)}) %all-reduce.3.cloned.1.call-update) | async-done | bytes 3145744 | tf_op jit(solution)/shard_map/psum | solution.py:123
  309.9 2.7 convert_element_type.124
  312.7 0.0 copy-start.1
  312.7 2.7 copy-done.1
  315.3 0.0 copy-done.5
  315.3 0.0 copy-done.6
  315.3 1.1 fusion.16
  316.4 0.0 all-gather.3.cloned.1.call-update
  316.4 0.0 all-gather.5.cloned.1.call-start
  316.5 0.7 all-gather.5.cloned.1.call-update
  317.2 0.0 copy-start.7
  317.2 3.0 multiply_convert_fusion.1
  320.2 0.0 copy-start.4
  320.2 0.0 copy-done.7
  320.2 1.2 fusion.14
  321.5 0.0 copy-done.4
  321.5 1.1 fusion.7
  322.5 2.7 add_convert_fusion
  325.3 4.6 all-to-all-start.3
  331.8 40.9 %all-to-all-done.3 = bf16[16,24,4096]{2,1,0:T(8,128)(2,1)} async-done(((bf16[16,24,4096]{2,1,0:T(8,128)(2,1)}), bf16[16,24,4096]{2,1,0:T(8,128)(2,1)}, u32[]{:S(2)}, u32[]{:S(2)}) %all-to-all-start.3) | async-done | bytes 3145760 | tf_op jit(solution)/shard_map/all_to_all | solution.py:106
  372.8 4.1 convolution_convert_fusion
  376.8 43.8 %all-gather.3.cloned.1.call-done = bf16[2,192,4096]{2,1,0:T(8,128)(2,1)} async-done(((bf16[2,192,256]{2,1,0:T(8,128)(2,1)}), bf16[2,192,4096]{2,1,0:T(8,128)(2,1)}) %all-gather.3.cloned.1.call-update) | async-done | bytes 3145744 | tf_op jit(solution)/shard_map/all_gather | solution.py:125
  420.7 94.2 %all-gather.5.cloned.1.call-done = bf16[2,192,4096]{2,1,0:T(8,128)(2,1)} async-done(((bf16[2,192,256]{2,1,0:T(8,128)(2,1)}), bf16[2,192,4096]{2,1,0:T(8,128)(2,1)}) %all-gather.5.cloned.1.call-update) | async-done | bytes 3145744 | tf_op jit(solution)/shard_map/all_gather | solution.py:128
  514.8 6.1 %fusion.6 = bf16[1,192,4096]{2,1,0:T(8,128)(2,1)} fusion(f32[2,192,4096]{2,1,0:T(8,128)} %copy-done.1, s32[]{:T(128)S(6)} %select_n.25, bf16[2,192,4096]{2,1,0:T(8,128)(2,1)} %all-gather.5.cloned.1.call-done, bf16[2,192,4096]{2,1,0:T(8,128)(2,1)} %all-gather.3.cloned.1.call-done), kind=kLoop, calls=%fused_computation.14 | loop fusion | flops 10223616 | bytes 7864324 | tf_op jit(solution)/shard_map/convert_element_type | solution.py:141
  (15 shorter events, 0.2 us)
Async XLA Ops:
  7.2 74.0 %copy-start = (bf16[1,4096,192]{1,2,0:T(8,128)(2,1)S(1)}, bf16[1,4096,192]{1,2,0:T(8,128)(2,1)}, u32[]{:S(2)}) copy-start(bf16[1,4096,192]{1,2,0:T(8,128)(2,1)} %param.14) | copy-start | bytes 4718596
  11.9 10.5 %all-to-all-start = ((bf16[16,1,24]{2,1,0:T(2,128)(2,1)}), bf16[16,1,24]{2,1,0:T(2,128)(2,1)S(1)}, u32[]{:S(2)}, u32[]{:S(2)}) async-start(bf16[16,1,24]{2,1,0:T(2,128)(2,1)} %copy.29), calls=%async_computation | async-start | bytes 16384 | tf_op jit(solution)/shard_map/all_to_all | solution.py:75
  24.5 48.6 %all-to-all-start.2 = ((bf16[16,24,4096]{2,1,0:T(8,128)(2,1)}), bf16[16,24,4096]{2,1,0:T(8,128)(2,1)}, u32[]{:S(2)}, u32[]{:S(2)}) async-start(bf16[16,24,4096]{2,1,0:T(8,128)(2,1)} %bitcast.62), calls=%async_computation.2 | async-start | bytes 6291456 | tf_op jit(solution)/shard_map/all_to_all | solution.py:73
  75.1 4.6 copy-start.8
  75.2 47.2 %all-to-all-start.1 = ((bf16[16,24,4096]{2,1,0:T(8,128)(2,1)}), bf16[16,24,4096]{2,1,0:T(8,128)(2,1)}, u32[]{:S(2)}, u32[]{:S(2)}) async-start(bf16[16,24,4096]{2,1,0:T(8,128)(2,1)} %bitcast.60), calls=%async_computation.1 | async-start | bytes 6291456 | tf_op jit(solution)/shard_map/all_to_all | solution.py:74
  79.7 4.5 copy-start.2
  79.7 230.2 %all-reduce.3.cloned.1.call-start = ((), (), s32[]{:S(2)}) async-start(), calls=%async_computation.5 | async-start | bytes 6291456 | tf_op jit(solution)/shard_map/psum | solution.py:123
  122.3 2.9 copy-start.3
  128.5 292.1 %all-gather.3.cloned.1.call-start = ((), (), s32[]{:S(2)}) async-start(), calls=%async_computation.4 | async-start | bytes 3342336 | tf_op jit(solution)/shard_map/all_gather | solution.py:125
  309.9 5.4 %copy-start.5 = (f32[2,192,256]{2,1,0:T(8,128)S(1)}, f32[2,192,256]{2,1,0:T(8,128)}, u32[]{:S(2)}) copy-start(f32[2,192,256]{2,1,0:T(8,128)} %param.19) | copy-start | bytes 1179652
  309.9 5.4 %copy-start.6 = (f32[2,192,256]{2,1,0:T(8,128)S(1)}, f32[2,192,256]{2,1,0:T(8,128)}, u32[]{:S(2)}) copy-start(f32[2,192,256]{2,1,0:T(8,128)} %param.18) | copy-start | bytes 1179652
  312.7 2.7 copy-start.1
  316.4 198.4 %all-gather.5.cloned.1.call-start = ((), (), s32[]{:S(2)}) async-start(), calls=%async_computation.6 | async-start | bytes 3342336 | tf_op jit(solution)/shard_map/all_gather | solution.py:128
  317.2 3.0 copy-start.7
  320.2 1.2 copy-start.4
  325.3 47.5 %all-to-all-start.3 = ((bf16[16,24,4096]{2,1,0:T(8,128)(2,1)}), bf16[16,24,4096]{2,1,0:T(8,128)(2,1)}, u32[]{:S(2)}, u32[]{:S(2)}) async-start(bf16[16,24,4096]{2,1,0:T(8,128)(2,1)} %bitcast.61), calls=%async_computation.3 | async-start | bytes 6291456 | tf_op jit(solution)/shard_map/all_to_all | solution.py:106
Sparse Core Ops, SparseCore 0:
  128.7 181.2 all-reduce.2
  316.6 104.0 all-gather.2
  423.1 91.6 all-gather.4
where the time goes:
time: 528 us; the launch traced here: 527 us
  waiting for transfers between devices  439 us (83%)
  other arithmetic  22.7 us (4%)
  starting transfers between devices  20.7 us (4%)
  matrix products  20.5 us (4%)
  between operations  16 us (3%)
  local copies, waits for them, and re-layouts  8.52 us (2%)
    psum x1, waiting for transfers between devices, body(): lax.psum(cand_grads.astype(jnp.bfloat16), 'grp').astype(jnp.float32)  181 us
    all_gather x1, waiting for transfers between devices, body(): lax.all_gather(moment_second.astype(jnp.bfloat16), 'grp', axis=2, tiled=T...  94.2 us
    all_gather x1, waiting for transfers between devices, body(): lax.all_gather(moment_first.astype(jnp.bfloat16), 'grp', axis=2, tiled=True)  43.8 us
    all_to_all x1, waiting for transfers between devices, body(): lax.all_to_all(spread(send_tokens), 'ep', split_axis=0, concat_axis=0, ti...  41.2 us
    all_to_all x1, waiting for transfers between devices, body(): lax.all_to_all(partial_value.reshape(num_ep, CAP, width), 'ep', split_axi...  40.9 us
    all_to_all x1, waiting for transfers between devices, body(): lax.all_to_all(spread(send_grads), 'ep', split_axis=0, concat_axis=0, til...  34.3 us
  transfers between devices with their start and end apart: 7, of which 7 were waited for; matrix products, arithmetic and copies ran while one was open for 5% of the time, Pallas kernels for 0%

commit v1 on v0

--- a/solution.py
+++ b/solution.py
@@ -12,6 +12,18 @@
 adam_eps = 1e-08
 first_fix = 1.0 - math.exp(1000.0 * math.log(0.9))
 second_fix = 1.0 - math.exp(1000.0 * math.log(0.999))
+
+
+def close_edges(payload, mesh_name="grp"):
+    return jnp.concatenate(
+        lax.all_to_all(
+            jnp.stack([payload] * lax.axis_size(mesh_name), axis=0),
+            mesh_name,
+            split_axis=0,
+            concat_axis=0,
+        ),
+        axis=2,
+    )
 
 
 def moments(gradient, first_moment, second):
@@ -122,9 +134,7 @@
     cand_grads = cand_mask[:, None, None] * weight_grad[None]
     totals = lax.psum(cand_grads.astype(jnp.bfloat16), "grp").astype(jnp.float32)
     full_first, full_second = (
-        lax.all_gather(moment_first.astype(jnp.bfloat16), "grp", axis=2, tiled=True).astype(
-            moment_first.dtype
-        ),
+        close_edges(moment_first.astype(jnp.bfloat16)).astype(moment_first.dtype),
         lax.all_gather(moment_second.astype(jnp.bfloat16), "grp", axis=2, tiled=True).astype(
             moment_second.dtype
         ),

time: 528 us -> 502 us (0.951)
  waiting for transfers between devices: 439 us -> 393 us
  local copies, waits for them, and re-layouts: 8.52 us -> 15.7 us
  matrix products: 20.5 us -> 25.9 us
    all_to_all x0 -> x1, waiting for transfers between devices: none -> 65.9 us  [close_edges(): lax.all_to_all(jnp.stack([payload] * lax.axis_size(mesh_name), axis=0), m...]
    all_gather x1, waiting for transfers between devices: 94.2 us -> 47.7 us  [body(): lax.all_gather(moment_second.astype(jnp.bfloat16), 'grp', axis=2, tiled=T...]
    all_gather x1 -> x0, waiting for transfers between devices: 43.8 us -> none  [body(): lax.all_gather(moment_first.astype(jnp.bfloat16), 'grp', axis=2, tiled=True)]
    all_to_all x1, waiting for transfers between devices: 40.9 us -> 0.01 us  [body(): lax.all_to_all(partial_value.reshape(num_ep, CAP, width), 'ep', split_axi...]
    psum x1, waiting for transfers between devices: 181 us -> 200 us  [body(): lax.psum(cand_grads.astype(jnp.bfloat16), 'grp').astype(jnp.float32)]
  transfers between devices with their start and end apart: 7 -> 7, of which waited for: 7 -> 6; matrix products, arithmetic and copies ran while one was open for 5% -> 6% of each run, Pallas kernels for 0% -> 0%
where the time goes in v1:
time: 502 us
  waiting for transfers between devices  393 us (78%)
  matrix products  25.9 us (5%)
  other arithmetic  25.6 us (5%)
  starting transfers between devices  25.6 us (5%)
  between operations  16.3 us (3%)
  local copies, waits for them, and re-layouts  15.7 us (3%)
    psum x1, waiting for transfers between devices, body(): lax.psum(cand_grads.astype(jnp.bfloat16), 'grp').astype(jnp.float32)  200 us
    all_to_all x1, waiting for transfers between devices, close_edges(): lax.all_to_all(jnp.stack([payload] * lax.axis_size(mesh_name), axis=0), m...  65.9 us
    all_gather x1, waiting for transfers between devices, body(): lax.all_gather(moment_second.astype(jnp.bfloat16), 'grp', axis=2, tiled=T...  47.7 us
    all_to_all x1, waiting for transfers between devices, body(): lax.all_to_all(spread(send_tokens), 'ep', split_axis=0, concat_axis=0, ti...  41.1 us
    all_to_all x1, waiting for transfers between devices, body(): lax.all_to_all(spread(send_grads), 'ep', split_axis=0, concat_axis=0, til...  34.3 us
  transfers between devices with their start and end apart: 7, of which 6 were waited for; matrix products, arithmetic and copies ran while one was open for 6% of the time, Pallas kernels for 0%

profile of v1, /device:TPU:2, one launch (start us, length us, event | category | flops | bytes accessed | tf_op | source)
XLA Modules:
  0.0 501.6 jit_solution(17101681857297368069)
XLA Ops:
  7.2 0.0 copy-start
  7.2 0.8 bitcast_add_fusion
  8.0 0.8 compare_reduce_fusion
  8.8 1.2 reduce-window.6
  10.0 0.1 slice.12
  10.1 0.1 copy.28
  10.2 0.1 copy.29
  10.3 0.1 add_bitcast_fusion
  10.4 0.8 fusion.24
  11.2 0.1 select_reduce_fusion
  11.3 0.6 copy.30
  11.9 5.9 %all-to-all-start = ((bf16[16,1,24]{2,1,0:T(2,128)(2,1)}), bf16[16,1,24]{2,1,0:T(2,128)(2,1)S(1)}, u32[]{:S(2)}, u32[]{:S(2)}) async-start(bf16[16,1,24]{2,1,0:T(2,128)(2,1)} %copy.30), calls=%async_computation | async-start | bytes 16384 | tf_op jit(solution)/shard_map/all_to_all | solution.py:87
  17.8 0.1 eq.59
  17.9 0.1 fusion.21
  18.0 1.8 convolution_convert_fusion.1
  19.8 2.6 all-to-all-done
  22.4 2.1 broadcast_in_dim.53
  24.5 5.7 %all-to-all-start.2 = ((bf16[16,24,4096]{2,1,0:T(8,128)(2,1)}), bf16[16,24,4096]{2,1,0:T(8,128)(2,1)}, u32[]{:S(2)}, u32[]{:S(2)}) async-start(bf16[16,24,4096]{2,1,0:T(8,128)(2,1)} %bitcast.67), calls=%async_computation.2 | async-start | bytes 6291456 | tf_op jit(solution)/shard_map/all_to_all | solution.py:85
  30.1 1.8 convolution_convert_fusion.2
  31.9 41.1 %all-to-all-done.2 = bf16[16,24,4096]{2,1,0:T(8,128)(2,1)} async-done(((bf16[16,24,4096]{2,1,0:T(8,128)(2,1)}), bf16[16,24,4096]{2,1,0:T(8,128)(2,1)}, u32[]{:S(2)}, u32[]{:S(2)}) %all-to-all-start.2) | async-done | bytes 3145760 | tf_op jit(solution)/shard_map/all_to_all | solution.py:85
  73.1 2.1 broadcast_in_dim.29
  75.1 4.5 all-to-all-start.1
  79.7 0.0 copy-start.3
  79.7 0.0 all-reduce.3.cloned.1.call-start
  79.7 0.0 copy-done.10
  79.8 0.6 constant_dynamic-slice_fusion
  80.3 0.6 compare_convert_fusion
  81.0 0.1 reshape.127
  81.1 0.0 copy-done
  81.1 3.1 fusion.9
  84.2 0.0 copy-done.3
  84.2 3.8 fusion.12
  88.0 34.3 %all-to-all-done.1 = bf16[16,24,4096]{2,1,0:T(8,128)(2,1)} async-done(((bf16[16,24,4096]{2,1,0:T(8,128)(2,1)}), bf16[16,24,4096]{2,1,0:T(8,128)(2,1)}, u32[]{:S(2)}, u32[]{:S(2)}) %all-to-all-start.1) | async-done | bytes 3145760 | tf_op jit(solution)/shard_map/all_to_all | solution.py:86
  122.3 3.0 multiply_convert_fusion.1
  125.3 0.0 copy-start.6
  125.3 0.0 copy-done.9
  125.3 1.2 fusion.14
  126.5 0.0 copy-start.4
  126.5 0.7 copy-done.4
  127.2 3.7 fusion.7
  131.0 2.9 fusion
  133.9 1.0 fusion.18
  134.9 2.3 multiply_convert_fusion
  137.1 0.0 all-reduce.3.cloned.1.call-update
  137.1 0.9 copy-done.5
  138.1 5.5 %add_convert_fusion = bf16[384,4096]{1,0:T(8,128)(2,1)} fusion(f32[384,4096]{1,0:T(8,128)} %fusion.7, bf16[1,4096,192]{1,2,0:T(8,128)(2,1)S(1)} %copy-done.3, f32[384,192]{0,1:T(8,128)S(1)} %copy-done.5, f32[384,192]{0,1:T(8,128)S(1)} %fusion.9), kind=kOutput, calls=%fused_computation.4 | convolution fusion | flops 607567872 | bytes 11599872 | tf_op jit(solution)/shard_map/rh,dh->rd/dot_general | solution.py:116
  143.6 4.4 all-to-all-start.3
  148.0 0.0 copy-start.7
  148.0 0.0 copy-start.8
  148.0 200.4 %all-reduce.3.cloned.1.call-done = bf16[2,192,4096]{2,1,0:T(8,128)(2,1)} async-done(((bf16[2,192,4096]{2,1,0:T(8,128)(2,1)}), bf16[2,192,4096]{2,1,0:T(8,128)(2,1)}) %all-reduce.3.cloned.1.call-update) | async-done | bytes 3145744 | tf_op jit(solution)/shard_map/psum | solution.py:135
  348.3 2.6 convert_element_type.132
  351.0 2.7 copy-done.2
  353.7 1.0 fusion.16
  354.7 0.0 all-to-all-done.3
  354.7 2.0 stack.2
  356.7 4.9 all-to-all-start.4
  361.6 0.2 all-gather.2.cloned.1.call-start
  361.8 0.5 all-gather.2.cloned.1.call-update
  364.3 4.1 convolution_convert_fusion
  368.4 65.9 %all-to-all-done.4 = bf16[16,2,192,256]{3,2,1,0:T(8,128)(2,1)} async-done(((bf16[16,2,192,256]{3,2,1,0:T(8,128)(2,1)}), bf16[16,2,192,256]{3,2,1,0:T(8,128)(2,1)}, u32[]{:S(2)}, u32[]{:S(2)}) %all-to-all-start.4) | async-done | bytes 3145760 | tf_op jit(solution)/shard_map/all_to_all | solution.py:19
  434.3 2.7 convert_bitcast_fusion
  437.0 3.5 copy.32
  440.5 47.7 %all-gather.2.cloned.1.call-done = bf16[2,192,4096]{2,1,0:T(8,128)(2,1)} async-done(((bf16[2,192,256]{2,1,0:T(8,128)(2,1)}), bf16[2,192,4096]{2,1,0:T(8,128)(2,1)}) %all-gather.2.cloned.1.call-update) | async-done | bytes 3145744 | tf_op jit(solution)/shard_map/all_gather | solution.py:138
  488.2 6.5 %fusion.6 = bf16[1,192,4096]{2,1,0:T(8,128)(2,1)} fusion(f32[2,192,4096]{2,1,0:T(8,128)} %copy-done.2, s32[]{:T(128)S(6)} %select_n.25, f32[2,192,4096]{2,1,0:T(8,128)} %bitcast.64, bf16[2,192,4096]{2,1,0:T(8,128)(2,1)} %all-gather.2.cloned.1.call-done), kind=kLoop, calls=%fused_computation.15 | loop fusion | flops 9437184 | bytes 9437188 | tf_op jit(solution)/shard_map/convert_element_type | solution.py:151
  (21 shorter events, 0.2 us)
Async XLA Ops:
  7.2 74.0 %copy-start = (bf16[1,4096,192]{1,2,0:T(8,128)(2,1)S(1)}, bf16[1,4096,192]{1,2,0:T(8,128)(2,1)}, u32[]{:S(2)}) copy-start(bf16[1,4096,192]{1,2,0:T(8,128)(2,1)} %param.14) | copy-start | bytes 4718596
  11.9 10.5 %all-to-all-start = ((bf16[16,1,24]{2,1,0:T(2,128)(2,1)}), bf16[16,1,24]{2,1,0:T(2,128)(2,1)S(1)}, u32[]{:S(2)}, u32[]{:S(2)}) async-start(bf16[16,1,24]{2,1,0:T(2,128)(2,1)} %copy.30), calls=%async_computation | async-start | bytes 16384 | tf_op jit(solution)/shard_map/all_to_all | solution.py:87
  24.5 48.6 %all-to-all-start.2 = ((bf16[16,24,4096]{2,1,0:T(8,128)(2,1)}), bf16[16,24,4096]{2,1,0:T(8,128)(2,1)}, u32[]{:S(2)}, u32[]{:S(2)}) async-start(bf16[16,24,4096]{2,1,0:T(8,128)(2,1)} %bitcast.67), calls=%async_computation.2 | async-start | bytes 6291456 | tf_op jit(solution)/shard_map/all_to_all | solution.py:85
  75.1 4.6 copy-start.10
  75.1 47.2 %all-to-all-start.1 = ((bf16[16,24,4096]{2,1,0:T(8,128)(2,1)}), bf16[16,24,4096]{2,1,0:T(8,128)(2,1)}, u32[]{:S(2)}, u32[]{:S(2)}) async-start(bf16[16,24,4096]{2,1,0:T(8,128)(2,1)} %bitcast.65), calls=%async_computation.1 | async-start | bytes 6291456 | tf_op jit(solution)/shard_map/all_to_all | solution.py:86
  79.7 4.6 copy-start.3
  79.7 268.7 %all-reduce.3.cloned.1.call-start = ((), (), s32[]{:S(2)}) async-start(), calls=%async_computation.5 | async-start | bytes 6291456 | tf_op jit(solution)/shard_map/psum | solution.py:135
  122.3 3.0 copy-start.9
  125.3 1.9 copy-start.6
  126.5 0.7 copy-start.4
  137.1 1.0 copy-start.5
  143.6 211.1 %all-to-all-start.3 = ((bf16[16,24,4096]{2,1,0:T(8,128)(2,1)}), bf16[16,24,4096]{2,1,0:T(8,128)(2,1)}, u32[]{:S(2)}, u32[]{:S(2)}) async-start(bf16[16,24,4096]{2,1,0:T(8,128)(2,1)} %bitcast.66), calls=%async_computation.3 | async-start | bytes 6291456 | tf_op jit(solution)/shard_map/all_to_all | solution.py:118
  148.0 205.7 %copy-start.7 = (f32[2,192,256]{2,1,0:T(8,128)S(1)}, f32[2,192,256]{2,1,0:T(8,128)}, u32[]{:S(2)}) copy-start(f32[2,192,256]{2,1,0:T(8,128)} %param.19) | copy-start | bytes 1179652
  148.0 205.7 %copy-start.8 = (f32[2,192,256]{2,1,0:T(8,128)S(1)}, f32[2,192,256]{2,1,0:T(8,128)}, u32[]{:S(2)}) copy-start(f32[2,192,256]{2,1,0:T(8,128)} %param.18) | copy-start | bytes 1179652
  351.0 2.7 copy-start.2
  356.7 77.6 %all-to-all-start.4 = ((bf16[16,2,192,256]{3,2,1,0:T(8,128)(2,1)}), bf16[16,2,192,256]{3,2,1,0:T(8,128)(2,1)}, u32[]{:S(2)}, u32[]{:S(2)}) async-start(bf16[16,2,192,256]{3,2,1,0:T(8,128)(2,1)} %stack.2), calls=%async_computation.4 | async-start | bytes 6291456 | tf_op jit(solution)/shard_map/all_to_all | solution.py:19
  361.6 126.6 %all-gather.2.cloned.1.call-start = ((), (), s32[]{:S(2)}) async-start(), calls=%async_computation.6 | async-start | bytes 3342336 | tf_op jit(solution)/shard_map/all_gather | solution.py:138
  488.2 6.5 %copy-start.1 = (bf16[1,4096,192]{1,2,0:T(8,128)(2,1)S(1)}, bf16[1,4096,192]{1,2,0:T(8,128)(2,1)}, u32[]{:S(2)}) copy-start(bf16[1,4096,192]{1,2,0:T(8,128)(2,1)} %param.14) | copy-start | bytes 4718596
Sparse Core Ops, SparseCore 0:
  137.3 211.0 all-reduce.2
  365.5 122.7 all-gather.1
